TPU v7x, 1024 devices: a whole 8x8x8 slice. The times are simulated.
1024 devices in a mesh: row: 32 (over x, z_hi, core), col: 32 (over y, z_lo).
Axes of the slice: x: 8, y: 8, z: 8 (z_hi: 2, z_lo: 4; z = z_hi * 4 + z_lo), core: 2. Of those that a mesh axis runs over, the one named last changes fastest.
Arguments:
- iterate: bfloat16 [3584, 16384], P('row', 'col'), may hold values from -0.046875 to 0.046875
- weight: float32 [3584, 16384], P('row', 'col'), may hold values from -0.625 to 0.625
Outputs:
- update: float32 [3584, 16384], P('row', 'col')
- new_weight: float32 [3584, 16384], P('row', 'col')
All inputs are finite; a program needn't handle non-finite values.
Results may differ from a plain program's by a relative error of at most 0.04.
Values may be sent and summed in bfloat16 or wider, within the bound.
A program may use at most 32 MiB of HBM per device.

v0:
```python
import math

import jax
import jax.numpy as jnp
from jax import lax
from jax.sharding import PartitionSpec as P

M = 3584
N = 16384


poly_one = 3.4445
poly_three = -4.775
poly_five = 2.0315
learn_rate = 0.02
decay_rate = 0.1


def cross_rows(left, right):
    return lax.dot_general(
        left, right, (((1,), (1,)), ((), ())), preferred_element_type=jnp.float32
    )


def shards(iterate, weight):
    column_panel = lax.all_gather(iterate, "row", axis=0, tiled=True)
    piece = column_panel
    gram_swapped = lax.psum_scatter(
        cross_rows(piece, iterate), "col", scatter_dimension=0, tiled=True
    )
    gram = gram_swapped.T.astype(jnp.bfloat16)
    gram_panel = lax.all_gather(gram, "row", axis=0, tiled=True)
    piece = gram_panel
    square = lax.psum_scatter(cross_rows(piece, gram), "col", scatter_dimension=0, tiled=True).T
    poly = (poly_three * gram.astype(jnp.float32) + poly_five * square).astype(jnp.bfloat16)
    poly_panel = lax.all_gather(poly, "col", axis=1, tiled=True)
    following = poly_one * iterate.astype(jnp.float32) + jnp.dot(
        poly_panel, column_panel, preferred_element_type=jnp.float32
    )
    update = 0.2 * math.sqrt(max(M, N)) * following
    new_weight = weight * (1.0 - learn_rate * decay_rate) - learn_rate * update
    return (update, new_weight)


def solution(mesh):
    in_specs = (P("row", "col"), P("row", "col"))
    out_specs = (P("row", "col"), P("row", "col"))
    return jax.shard_map(shards, mesh=mesh, in_specs=in_specs, out_specs=out_specs, check_vma=False)
```

profile of v0, /device:TPU:2, one launch (start us, length us, event | category | flops | bytes accessed | tf_op | source)
XLA Modules:
  0.0 608.5 jit_solution(10768230801263070138)
XLA Ops:
  7.2 0.0 all-gather.2.cloned.1.call-start
  7.2 0.7 all-gather.2.cloned.1.call-update
  7.9 0.0 reduce-scatter.3.cloned.1.call-start
  7.9 125.3 %all-gather.2.cloned.1.call-done = bf16[3584,512]{1,0:T(8,128)(2,1)} async-done(((bf16[112,512]{1,0:T(8,128)(2,1)}), bf16[3584,512]{1,0:T(8,128)(2,1)}) %all-gather.2.cloned.1.call-update) | async-done | bytes 3670032 | tf_op jit(solution)/shard_map/all_gather | solution.py:26
  133.3 4.4 fusion.3
  137.7 0.0 reduce-scatter.3.cloned.1.call-update
  137.7 0.0 copy-start
  137.7 0.0 copy-start.2
  137.7 0.0 reduce-scatter.5.cloned.1.call-start
  137.8 161.8 %reduce-scatter.3.cloned.1.call-done = f32[112,112]{1,0:T(8,128)} async-done(((f32[3584,112]{1,0:T(8,128)}), f32[112,112]{1,0:T(8,128)}) %reduce-scatter.3.cloned.1.call-update) | async-done | bytes 50192 | tf_op jit(solution)/shard_map/reduce_scatter | solution.py:28
  299.6 0.0 copy-start.1
  299.6 0.9 convert_bitcast_fusion
  300.5 0.1 copy.4
  300.6 53.2 %all_gather.10 = bf16[3584,112]{1,0:T(8,128)(2,1)S(1)} all-gather(bf16[112,112]{1,0:T(8,128)(2,1)S(1)} %copy.4), channel_id=1, replica_groups=mesh['row'=32,'col'=32] {'row'}, dimensions={0}, use_global_device_ids=true | all-gather | bytes 827904 | tf_op jit(solution)/shard_map/all_gather | solution.py:32
  353.8 2.5 fusion.1
  356.2 0.0 reduce-scatter.5.cloned.1.call-update
  356.2 162.2 %reduce-scatter.5.cloned.1.call-done = f32[112,112]{1,0:T(8,128)} async-done(((f32[3584,112]{1,0:T(8,128)}), f32[112,112]{1,0:T(8,128)}) %reduce-scatter.5.cloned.1.call-update) | async-done | bytes 50192 | tf_op jit(solution)/shard_map/reduce_scatter | solution.py:34
  518.5 0.0 copy-done.1
  518.5 0.8 fusion
  519.3 79.0 %all_gather.11 = bf16[112,3584]{0,1:T(8,128)(2,1)S(1)} all-gather(bf16[112,112]{0,1:T(8,128)(2,1)S(1)} %fusion), channel_id=1, replica_groups=mesh['row'=32,'col'=32] {'col'}, dimensions={1}, use_global_device_ids=true | all-gather | bytes 827904 | tf_op jit(solution)/shard_map/all_gather | solution.py:36
  598.3 0.0 copy-done
  598.3 0.0 copy-done.2
  598.3 3.6 multiply_subtract_fusion
Async XLA Ops:
  7.2 126.1 %all-gather.2.cloned.1.call-start = ((), (), s32[]{:S(2)}) async-start(), calls=%async_computation.2 | async-start | bytes 3784704 | tf_op jit(solution)/shard_map/all_gather | solution.py:26
  7.9 291.7 %reduce-scatter.3.cloned.1.call-start = ((), (), s32[]{:S(2)}) async-start(), calls=%async_computation.3 | async-start | bytes 1892352 | tf_op jit(solution)/shard_map/reduce_scatter | solution.py:28
  137.7 460.7 %copy-start = (bf16[112,512]{1,0:T(8,128)(2,1)S(1)}, bf16[112,512]{1,0:T(8,128)(2,1)}, u32[]{:S(2)}) copy-start(bf16[112,512]{1,0:T(8,128)(2,1)} %param.2) | copy-start | bytes 344068
  137.7 460.6 %copy-start.2 = (f32[112,512]{1,0:T(8,128)S(1)}, f32[112,512]{1,0:T(8,128)}, u32[]{:S(2)}) copy-start(f32[112,512]{1,0:T(8,128)} %param.3) | copy-start | bytes 688132
  137.7 380.8 %reduce-scatter.5.cloned.1.call-start = ((), (), s32[]{:S(2)}) async-start(), calls=%async_computation.4 | async-start | bytes 1892352 | tf_op jit(solution)/shard_map/reduce_scatter | solution.py:34
  299.6 218.9 %copy-start.1 = (f32[112,112]{1,0:T(8,128)S(1)}, f32[112,112]{1,0:T(8,128)}, u32[]{:S(2)}) copy-start(f32[112,112]{1,0:T(8,128)} %reduce-scatter.3.cloned.1.call-done) | copy-start | bytes 150532
Sparse Core Ops, SparseCore 0:
  12.5 120.7 all-gather.1
  137.8 161.7 reduce-scatter.2
  356.4 162.0 reduce-scatter.4
where the time goes:
time: 609 us; the launch traced here: 608 us
  waiting for transfers between devices  450 us (74%)
  blocking collectives  132 us (22%)
  between operations  13.8 us (2%)
  matrix products  10.5 us (2%)
    reduce_scatter x1, waiting for transfers between devices, shards(): lax.psum_scatter(cross_rows(piece, gram), 'col', scatter_dimension=0, til...  162 us
    reduce_scatter x1, waiting for transfers between devices, shards(): lax.psum_scatter(cross_rows(piece, iterate), 'col', scatter_dimension=0,...  162 us
    all_gather x1, waiting for transfers between devices, shards(): column_panel = lax.all_gather(iterate, 'row', axis=0, tiled=True)  125 us
    all_gather x1, blocking collectives, shards(): poly_panel = lax.all_gather(poly, 'col', axis=1, tiled=True)  79 us
    all_gather x1, blocking collectives, shards(): gram_panel = lax.all_gather(gram, 'row', axis=0, tiled=True)  53.2 us
  transfers between devices with their start and end apart: 3, of which 3 were waited for; matrix products, arithmetic and copies ran while one was open for 0% of the time, Pallas kernels for 0%

commit v1 on v0

v1 whole, which is shorter than its diff:
```python
import math

import jax
import jax.numpy as jnp
from jax import lax
from jax.experimental import pallas as pl
from jax.experimental.pallas import tpu as pltpu
from jax.sharding import PartitionSpec as P

M = 3584
N = 16384

poly_one = 3.4445
poly_three = -4.775
poly_five = 2.0315
learn_rate = 0.02
decay_rate = 0.1

ROWS = 112
WIDE = 128
COLS = 512
NR = 32
NC = 32
MESH = pl.DeviceIdType.MESH
F32 = jnp.float32
BF16 = jnp.bfloat16


def owner_of(slot):
    b, q = slot // 4, slot % 4
    return (2 * q + b % 2) * 4 + (q + b // 2) % 4


def slot_of(col):
    y, zl = col // 4, col % 4
    q = y // 2
    return 4 * (2 * ((zl + 4 - q) % 4) + y % 2) + q


def kernel(
    x_ref, w_ref, up_ref, nw_ref,
    xp, wp, part, prec, gram, wacc, yacc, wbf,
    rx, fx, bx, cx, ox,
    rw, fw, bw, cw, ow,
    r2, s2, r3, s3,
):
    r = lax.axis_index("row")
    c = lax.axis_index("col")
    x, zh, k = r // 4, (r // 2) % 2, r % 2

    def slot(dx, same_zh, same_core=True):
        px = (x + dx + 8) % 8
        pz = zh if same_zh else 1 - zh
        pk = k if same_core else 1 - k
        return px * 4 + pz * 2 + pk

    ahead = (slot(1, True), c)
    behind = (slot(-1, True), c)
    across = (slot(0, False), c)
    twin = (slot(0, True, False), c)

    barrier = pltpu.get_barrier_semaphore()
    for device in (ahead, behind, across, twin):
        pl.semaphore_signal(barrier, inc=1, device_id=device, device_id_type=MESH)

    def greet(i, carry):
        pl.semaphore_signal(barrier, inc=1, device_id=(r, (c + i) % NC), device_id_type=MESH)
        return carry

    lax.fori_loop(1, NC, greet, 0)
    zeros = jnp.zeros((NR, WIDE - ROWS, COLS), BF16)
    xp[:, ROWS:, :] = zeros
    wp[:, ROWS:, :] = zeros
    xp[r, :ROWS, :] = x_ref[...]
    pl.semaphore_wait(barrier, NC - 1 + 4)

    def ring(src, buf, recv, fsem, bsem, csem, osem, unit):
        def copy(source, s, send_sem, device):
            return pltpu.make_async_remote_copy(
                source, buf.at[s, pl.ds(0, ROWS)], send_sem, recv.at[s], device_id=device, device_id_type=MESH
            )

        started = []

        def send(source, s, send_sem, device):
            cp = copy(source, s, send_sem, device)
            cp.start()
            started.append(cp)

        def arrived(s):
            copy(buf.at[s, pl.ds(0, ROWS)], s, csem.at[s], twin).wait_recv()

        def forward(s, on_ahead, on_behind):
            here = buf.at[s, pl.ds(0, ROWS)]
            if on_ahead:
                send(here, s, fsem.at[s], ahead)
            if on_behind:
                send(here, s, bsem.at[s], behind)
            send(here, s, csem.at[s], twin)

        def pair(dx, same_zh):
            arrived(slot(dx, same_zh, False))
            unit(((x + dx + 8) % 8) * 2 + (zh if same_zh else 1 - zh))

        def both(d, same_zh, on_ahead, on_behind):
            lo, hi = slot(-d, same_zh), slot(d, same_zh)
            arrived(lo)
            forward(lo, on_ahead, False)
            arrived(hi)
            forward(hi, False, on_behind)

        send(src, r, osem.at[0], ahead)
        send(src, r, osem.at[1], behind)
        send(src, r, osem.at[2], across)
        send(src, r, osem.at[3], twin)
        pair(0, True)
        both(1, True, True, True)
        s = slot(0, False)
        arrived(s)
        forward(s, True, True)
        both(2, True, True, True)
        pair(-1, True)
        pair(1, True)
        both(1, False, True, True)
        pair(0, False)
        both(3, True, True, False)
        pair(-2, True)
        pair(2, True)
        both(2, False, True, True)
        pair(-1, False)
        pair(1, False)
        s = slot(-4, True)
        arrived(s)
        forward(s, False, False)
        pair(-3, True)
        pair(3, True)
        both(3, False, False, True)
        pair(-2, False)
        pair(2, False)
        s = slot(4, False)
        arrived(s)
        forward(s, False, False)
        pair(-4, True)
        pair(-3, False)
        pair(3, False)
        pair(4, False)
        return started

    mine = slot_of(c)

    def scatter(s):
        return pltpu.make_async_remote_copy(
            part.at[s], prec.at[c], s2.at[s], r2.at[c], device_id=(r, owner_of(s)), device_id_type=MESH
        )

    def gram_unit(p):
        rhs = xp[pl.ds(2 * p, 2)].reshape(2 * WIDE, COLS)
        res = lax.dot_general(x_ref[...], rhs, (((1,), (1,)), ((), ())), preferred_element_type=F32).astype(BF16)
        for h in range(2):
            s = 2 * p + h
            part[s] = res[:, h * WIDE : (h + 1) * WIDE]

            @pl.when(s != mine)
            def _():
                scatter(s).start()

    started = ring(x_ref, xp, rx, fx, bx, cx, ox, gram_unit)

    def add(i, total):
        o = (c + i) % NC
        pltpu.make_async_remote_copy(
            part.at[mine], prec.at[o], s2.at[mine], r2.at[o], device_id=(r, o), device_id_type=MESH
        ).wait_recv()
        return total + prec[o].astype(F32)

    total = lax.fori_loop(1, NC, add, part[mine].astype(F32))
    gram[mine] = total.astype(BF16)

    def spread(i):
        o = (c + i) % NC
        return pltpu.make_async_remote_copy(
            gram.at[mine], gram.at[mine], s3.at[i], r3.at[mine], device_id=(r, o), device_id_type=MESH
        )

    def spread_start(i, carry):
        spread(i).start()
        return carry

    lax.fori_loop(1, NC, spread_start, 0)

    for g in range(8):
        lhs, rhs = [], []
        for i in range(4 * g, 4 * g + 4):
            o = (c + NC - i) % NC
            s = slot_of(o)
            if i > 0:
                pltpu.make_async_remote_copy(
                    gram.at[s], gram.at[s], s3.at[i], r3.at[s], device_id=(r, o), device_id_type=MESH
                ).wait_recv()
            lhs.append(gram[s])
            rhs.append(xp[s])
        term = jnp.dot(jnp.concatenate(lhs, axis=1), jnp.concatenate(rhs, axis=0), preferred_element_type=F32)
        if g == 0:
            wacc[...] = term
        else:
            wacc[...] += term
    wbf[...] = wacc[...].astype(BF16)
    wp[r, :ROWS, :] = wbf[...]
    yacc[...] = jnp.zeros_like(yacc)

    def poly_unit(p):
        lhs = jnp.concatenate([gram[2 * p], gram[2 * p + 1]], axis=1)
        rhs = wp[pl.ds(2 * p, 2)].reshape(2 * WIDE, COLS)
        yacc[...] += jnp.dot(lhs, rhs, preferred_element_type=F32)

    started += ring(wbf, wp, rw, fw, bw, cw, ow, poly_unit)

    following = poly_one * x_ref[...].astype(F32) + poly_three * wacc[...] + poly_five * yacc[...]
    update = 0.2 * math.sqrt(max(M, N)) * following
    up_ref[...] = update
    nw_ref[...] = w_ref[...] * (1.0 - learn_rate * decay_rate) - learn_rate * update

    for cp in started:
        cp.wait_send()

    def drain(s, carry):
        @pl.when(s != mine)
        def _():
            scatter(s).wait_send()

        return carry

    lax.fori_loop(0, NR, drain, 0)

    def spread_drain(i, carry):
        spread(i).wait_send()
        return carry

    lax.fori_loop(1, NC, spread_drain, 0)


def shards(iterate, weight):
    dma = pltpu.SemaphoreType.DMA
    tile = jax.ShapeDtypeStruct((ROWS, COLS), F32)
    vmem = pl.BlockSpec(memory_space=pltpu.VMEM)
    return pl.pallas_call(
        kernel,
        out_shape=(tile, tile),
        in_specs=[vmem, vmem],
        out_specs=(vmem, vmem),
        scratch_shapes=[
            pltpu.VMEM((NR, WIDE, COLS), BF16),
            pltpu.VMEM((NR, WIDE, COLS), BF16),
            pltpu.VMEM((NR, ROWS, WIDE), BF16),
            pltpu.VMEM((NC, ROWS, WIDE), BF16),
            pltpu.VMEM((NR, ROWS, WIDE), BF16),
            pltpu.VMEM((ROWS, COLS), F32),
            pltpu.VMEM((ROWS, COLS), F32),
            pltpu.VMEM((ROWS, COLS), BF16),
        ]
        + [dma((NR,)), dma((NR,)), dma((NR,)), dma((NR,)), dma((4,))] * 2
        + [dma((NC,)), dma((NR,)), dma((NR,)), dma((NC,))],
        compiler_params=pltpu.CompilerParams(
            collective_id=0, has_side_effects=True, vmem_limit_bytes=32 * 2**20
        ),
        cost_estimate=pl.CostEstimate(flops=2 * 3 * ROWS * M * COLS, bytes_accessed=2**21, transcendentals=0),
    )(iterate, weight)


def solution(mesh):
    specs = (P("row", "col"), P("row", "col"))
    return jax.shard_map(shards, mesh=mesh, in_specs=specs, out_specs=specs, check_vma=False)
```

time: 609 us -> 142 us (0.23)
  the two profiles are of different devices: /device:TPU:2 before, /device:TPU:1 now
where the time goes in v1:
time: 142 us; the launch traced here: 140 us
  Pallas kernels  136 us (96%)
  local copies, waits for them, and re-layouts  3.21 us (2%)
    pallas_call x1, Pallas kernels, shards(): pl.pallas_call(kernel, out_shape=(tile, tile), in_specs=[vmem, vmem], out...  136 us
    unnamed x6, local copies, waits for them, and re-layouts  3.21 us

profile of v1, /device:TPU:1, one launch (start us, length us, event | category | flops | bytes accessed | tf_op | source)
XLA Modules:
  0.0 139.6 jit_solution(3208546602431603681)
XLA Ops:
  0.6 0.0 copy-start
  0.6 0.9 copy-done
  1.6 0.0 copy-start.1
  1.6 0.9 copy-done.1
  2.5 135.7 %shard_map.41 = (f32[112,512]{1,0:T(8,128)S(1)}, f32[112,512]{1,0:T(8,128)S(1)}) custom-call(bf16[112,512]{1,0:T(8,128)(2,1)S(1)} %copy-done.1, f32[112,512]{1,0:T(8,128)S(1)} %copy-done), custom_call_target="tpu_custom_call" | custom-call | flops 1233125376 | bytes 2097152 | tf_op jit(solution)/shard_map/pallas_call | solution.py:246
  138.2 0.7 copy.6
  138.9 0.7 copy.7
Async XLA Ops:
  0.6 0.9 copy-start
  1.6 0.9 copy-start.1

commit v2 on v0

v2 whole, which is shorter than its diff:
```python
import math

import jax
import jax.numpy as jnp
from jax import lax
from jax.experimental import pallas as pl
from jax.experimental.pallas import tpu as pltpu
from jax.sharding import PartitionSpec as P

M = 3584
N = 16384

poly_one = 3.4445
poly_three = -4.775
poly_five = 2.0315
learn_rate = 0.02
decay_rate = 0.1

ROWS = 112
WIDE = 128
COLS = 512
NR = 32
NY, NZ, NX = 8, 4, 8
CUT = 64
REST = ROWS - CUT
CHUNKS = ((0, CUT), (CUT, REST))
MESH = pl.DeviceIdType.MESH
F32 = jnp.float32
BF16 = jnp.bfloat16
AROUND = (0, 1, 7, 2, 6, 3, 5, 4)


def owner_of(slot):
    b, q = slot // 4, slot % 4
    return 2 * q + b % 2, (q + b // 2) % NZ


def slot_of(y, zl):
    q = y // 2
    return 4 * (2 * ((zl + NZ - q) % NZ) + y % 2) + q


def kernel(
    xv, out_ref,
    xp, part, pa, pb, sa, sb, qa, qb, gram, pol, bt, yacc,
    rx, fx, bx, cx, ox,
    rpa, rpb, spa, spb, rqa, rqb, sqa, sqb,
    ray, raz, say, saz, rby, rbz, sby, sbz,
    rt, st, ct, ot,
):
    r = lax.axis_index("row")
    c = lax.axis_index("col")
    x, zh, k = r // 4, (r // 2) % 2, r % 2
    y, zl = c // NZ, c % NZ

    def slot(dx, same_zh, same_core=True):
        px = (x + dx + NX) % NX
        pz = zh if same_zh else 1 - zh
        pk = k if same_core else 1 - k
        return px * 4 + pz * 2 + pk

    ahead = (slot(1, True), c)
    behind = (slot(-1, True), c)
    across = (slot(0, False), c)
    twin = (slot(0, True, False), c)

    def y_peer(i):
        return (y + i) % NY

    def z_peer(i):
        return (zl + i) % NZ

    barrier = pltpu.get_barrier_semaphore()
    peers = [across, twin]
    peers += [(slot(i, True), c) for i in range(1, NX)]
    peers += [(r, y_peer(i) * NZ + zl) for i in range(1, NY)]
    peers += [(r, y * NZ + z_peer(i)) for i in range(1, NZ)]
    for device in peers:
        pl.semaphore_signal(barrier, inc=1, device_id=device, device_id_type=MESH)
    xp[:, ROWS:, :] = jnp.zeros((NR, WIDE - ROWS, COLS), BF16)
    bt[:, ROWS:, :] = jnp.zeros((NR, WIDE - ROWS, WIDE), BF16)
    xp[r, :ROWS, :] = xv[...]
    pl.semaphore_wait(barrier, len(peers))

    def remote(src, dst, send_sem, recv_sem, device):
        return pltpu.make_async_remote_copy(src, dst, send_sem, recv_sem, device_id=device, device_id_type=MESH)

    def settle(ref, sem):
        pltpu.make_async_copy(ref, ref, sem).wait()

    started = []


    def send(source, s, h, send_sem, device):
        at, size = CHUNKS[h]
        cp = remote(source, xp.at[s, pl.ds(at, size)], send_sem, rx.at[s, h], device)
        cp.start()
        started.append(cp)

    def arrived(s, h):
        at, size = CHUNKS[h]
        settle(xp.at[s, pl.ds(at, size)], rx.at[s, h])

    def forward(s, h, on_ahead, on_behind):
        at, size = CHUNKS[h]
        here = xp.at[s, pl.ds(at, size)]
        if on_ahead:
            send(here, s, h, fx.at[s, h], ahead)
        if on_behind:
            send(here, s, h, bx.at[s, h], behind)
        send(here, s, h, cx.at[s, h], twin)

    def partial(dx, same_zh):
        other = slot(dx, same_zh, False)
        for h in range(2):
            arrived(other, h)
        p = other // 2
        rhs = xp[pl.ds(2 * p, 2)].reshape(2 * WIDE, COLS)
        res = lax.dot_general(xv[...], rhs, (((1,), (1,)), ((), ())), preferred_element_type=F32).astype(BF16)
        for h in range(2):
            s = 2 * p + h
            part[s] = res[:, h * WIDE : (h + 1) * WIDE]
            oy, oz = owner_of(s)

            @pl.when(oz != zl)
            def _():
                remote(part.at[s, pl.ds(0, CUT)], pa.at[zl, oy], spa, rpa, (r, y * NZ + oz)).start()

            @pl.when(oy != y)
            def _():
                remote(part.at[s, pl.ds(CUT, REST)], pb.at[y, oz], spb, rpb, (r, oy * NZ + zl)).start()

    def both(d, same_zh, on_ahead, on_behind):
        lo, hi = slot(-d, same_zh), slot(d, same_zh)
        for h in range(2):
            arrived(lo, h)
            forward(lo, h, on_ahead, False)
            arrived(hi, h)
            forward(hi, h, False, on_behind)

    def one(dx, same_zh, on_ahead, on_behind):
        s = slot(dx, same_zh)
        for h in range(2):
            arrived(s, h)
            forward(s, h, on_ahead, on_behind)

    for h, (at, size) in enumerate(CHUNKS):
        here = xv.at[pl.ds(at, size)]
        send(here, r, h, ox.at[2, h], across)
        send(here, r, h, ox.at[0, h], ahead)
        send(here, r, h, ox.at[1, h], behind)
        send(here, r, h, ox.at[3, h], twin)
    partial(0, True)
    both(1, True, True, True)
    one(0, False, True, True)
    both(2, True, True, True)
    partial(-1, True)
    partial(1, True)
    both(1, False, True, True)
    partial(0, False)
    both(3, True, True, False)
    partial(-2, True)
    partial(2, True)
    both(2, False, True, True)
    partial(-1, False)
    partial(1, False)
    one(-4, True, False, False)
    partial(-3, True)
    partial(3, True)
    both(3, False, False, True)
    partial(-2, False)
    partial(2, False)
    one(4, False, False, False)
    partial(-4, True)
    partial(-3, False)
    partial(3, False)
    partial(4, False)


    settle(pa.at[pl.ds(0, NZ - 1)], rpa)
    for i in AROUND:
        oy = y_peer(i)
        s = slot_of(oy, zl)
        total = part[s, :CUT].astype(F32)
        for j in range(1, NZ):
            total += pa[z_peer(j), oy].astype(F32)
        sa[i] = total.astype(BF16)
        if i:
            remote(sa.at[i], qa.at[y], sqa, rqa, (r, oy * NZ + zl)).start()
    settle(pb.at[pl.ds(0, NY - 1)], rpb)
    for j in range(NZ):
        oz = z_peer(j)
        s = slot_of(y, oz)
        total = part[s, CUT:].astype(F32)
        for i in range(1, NY):
            total += pb[y_peer(i), oz].astype(F32)
        sb[j] = total.astype(BF16)
        if j:
            remote(sb.at[j], qb.at[zl], sqb, rqb, (r, y * NZ + oz)).start()
    mine = slot_of(y, zl)
    settle(qa.at[pl.ds(0, NY - 1)], rqa)
    upper = sa[0].astype(F32)
    for i in range(1, NY):
        upper += qa[y_peer(i)].astype(F32)
    settle(qb.at[pl.ds(0, NZ - 1)], rqb)
    lower = sb[0].astype(F32)
    for j in range(1, NZ):
        lower += qb[z_peer(j)].astype(F32)
    gram[mine] = jnp.concatenate([upper, lower], axis=0).astype(BF16)


    def top(buf, s):
        return buf.at[s, pl.ds(0, CUT)]

    def low(buf, s):
        return buf.at[s, pl.ds(CUT, REST)]

    def spread(buf, n):
        def to_z(s):
            for j in range(1, NZ):
                remote(top(buf, s), top(buf, s), saz.at[n], raz.at[n, zl], (r, y * NZ + z_peer(j))).start()

        def to_y(s):
            for i in AROUND[1:]:
                remote(low(buf, s), low(buf, s), sby.at[n], rby.at[n, y], (r, y_peer(i) * NZ + zl)).start()

        for i in AROUND[1:]:
            remote(top(buf, mine), top(buf, mine), say.at[n], ray.at[n, y], (r, y_peer(i) * NZ + zl)).start()
        for j in range(1, NZ):
            remote(low(buf, mine), low(buf, mine), sbz.at[n], rbz.at[n, zl], (r, y * NZ + z_peer(j))).start()
        to_z(mine)
        to_y(mine)
        yield
        for j in range(1, NZ):
            s = slot_of(y, z_peer(j))
            settle(low(buf, s), rbz.at[n, z_peer(j)])
            to_y(s)
        for i in AROUND[1:]:
            s = slot_of(y_peer(i), zl)
            settle(top(buf, s), ray.at[n, y_peer(i)])
            to_z(s)

    def gathered(buf, n):
        for i in AROUND:
            oy = y_peer(i)
            if i == 0:
                for j in range(1, NZ):
                    settle(buf.at[pl.ds(0, NY), pl.ds(0, CUT)], raz.at[n, z_peer(j)])
            else:
                settle(buf.at[pl.ds(0, NZ), pl.ds(CUT, REST)], rby.at[n, oy])
            yield [slot_of(oy, z) for z in range(NZ)]

    def spread_done(buf, n):
        settle(buf.at[pl.ds(0, NY - 1), pl.ds(0, CUT)], say.at[n])
        settle(buf.at[pl.ds(0, NZ - 1), pl.ds(CUT, REST)], sbz.at[n])
        settle(buf.at[pl.ds(0, NY * (NZ - 1)), pl.ds(0, CUT)], saz.at[n])
        settle(buf.at[pl.ds(0, NZ * (NY - 1)), pl.ds(CUT, REST)], sby.at[n])

    def joined(buf, slots, axis):
        return jnp.concatenate([buf[s] for s in slots], axis=axis)

    steps = spread(gram, 0)
    next(steps)


    own = gram.at[mine]

    def tile(src, s, send_sem, device):
        cp = remote(src, bt.at[s, pl.ds(0, ROWS)], send_sem, rt.at[s], device)
        cp.start()
        started.append(cp)

    def tile_arrived(s):
        settle(bt.at[s, pl.ds(0, ROWS)], rt.at[s])

    bt[r, :ROWS] = gram[mine]
    tile(own, r, ot.at[0], across)
    for i in AROUND[1:]:
        tile(own, r, st.at[0, i], (slot(i, True), c))
    tile(own, r, ot.at[1], twin)
    for _ in steps:
        pass
    s = slot(0, False)
    tile_arrived(s)
    there = bt.at[s, pl.ds(0, ROWS)]
    for i in AROUND[1:]:
        tile(there, s, st.at[1, i], (slot(i, True), c))
    tile(there, s, ct.at[s], twin)
    for same in (True, False):
        for i in AROUND[1:]:
            s = slot(i, same)
            tile_arrived(s)
            tile(bt.at[s, pl.ds(0, ROWS)], s, ct.at[s], twin)
    for same in (True, False):
        for i in AROUND:
            tile_arrived(slot(i, same, False))

    square = jnp.zeros((ROWS, WIDE), F32)
    for slots in gathered(gram, 0):
        square += jnp.dot(joined(gram, slots, 1), joined(bt, slots, 0), preferred_element_type=F32)
    pol[mine] = (poly_three * gram[mine].astype(F32) + poly_five * square).astype(BF16)


    for _ in spread(pol, 1):
        pass
    yacc[...] = poly_one * xv[...].astype(F32)
    for slots in gathered(pol, 1):
        yacc[...] += jnp.dot(joined(pol, slots, 1), joined(xp, slots, 0), preferred_element_type=F32)
    out_ref[...] = yacc[...]

    for cp in started:
        cp.wait_send()
    settle(part.at[pl.ds(0, NY * (NZ - 1)), pl.ds(0, CUT)], spa)
    settle(part.at[pl.ds(0, NZ * (NY - 1)), pl.ds(CUT, REST)], spb)
    settle(sa.at[pl.ds(0, NY - 1)], sqa)
    settle(sb.at[pl.ds(0, NZ - 1)], sqb)
    spread_done(gram, 0)
    spread_done(pol, 1)


def shards(iterate, weight):
    dma = pltpu.SemaphoreType.DMA
    one = dma(())
    following = pl.pallas_call(
        kernel,
        out_shape=jax.ShapeDtypeStruct((ROWS, COLS), F32),
        in_specs=[pl.BlockSpec(memory_space=pltpu.VMEM)],
        out_specs=pl.BlockSpec(memory_space=pltpu.VMEM),
        scratch_shapes=[
            pltpu.VMEM((NR, WIDE, COLS), BF16),
            pltpu.VMEM((NR, ROWS, WIDE), BF16),
            pltpu.VMEM((NZ, NY, CUT, WIDE), BF16),
            pltpu.VMEM((NY, NZ, REST, WIDE), BF16),
            pltpu.VMEM((NY, CUT, WIDE), BF16),
            pltpu.VMEM((NZ, REST, WIDE), BF16),
            pltpu.VMEM((NY, CUT, WIDE), BF16),
            pltpu.VMEM((NZ, REST, WIDE), BF16),
            pltpu.VMEM((NR, ROWS, WIDE), BF16),
            pltpu.VMEM((NR, ROWS, WIDE), BF16),
            pltpu.VMEM((NR, WIDE, WIDE), BF16),
            pltpu.VMEM((ROWS, COLS), F32),
            dma((NR, 2)), dma((NR, 2)), dma((NR, 2)), dma((NR, 2)), dma((4, 2)),
            one, one, one, one, one, one, one, one,
            dma((2, NY)), dma((2, NZ)), dma((2,)), dma((2,)), dma((2, NY)), dma((2, NZ)), dma((2,)), dma((2,)),
            dma((NR,)), dma((2, NX)), dma((NR,)), dma((2,)),
        ],
        compiler_params=pltpu.CompilerParams(
            collective_id=0, has_side_effects=True, vmem_limit_bytes=32 * 2**20
        ),
        cost_estimate=pl.CostEstimate(flops=2 * 3 * ROWS * M * COLS, bytes_accessed=2**21, transcendentals=0),
    )(iterate)
    update = 0.2 * math.sqrt(max(M, N)) * following
    new_weight = weight * (1.0 - learn_rate * decay_rate) - learn_rate * update
    return (update, new_weight)


def solution(mesh):
    specs = (P("row", "col"), P("row", "col"))
    return jax.shard_map(shards, mesh=mesh, in_specs=specs, out_specs=specs, check_vma=False)
```

time: 609 us -> 98.3 us (0.16)
  the two profiles are of different devices: /device:TPU:2 before, /device:TPU:1 now
where the time goes in v2:
time: 98.3 us; the launch traced here: 98.2 us
  Pallas kernels  95.8 us (97%)
    pallas_call x1, Pallas kernels, shards(): pl.pallas_call(kernel, out_shape=jax.ShapeDtypeStruct((ROWS, COLS), F32),...  95.8 us

profile of v2, /device:TPU:1, one launch (start us, length us, event | category | flops | bytes accessed | tf_op | source)
XLA Modules:
  0.0 98.2 jit_solution(15694242584992201260)
XLA Ops:
  0.6 0.0 copy-start
  0.6 0.9 copy-done
  1.5 0.0 copy-start.1
  1.5 95.8 %shard_map.41 = f32[112,512]{1,0:T(8,128)S(1)} custom-call(bf16[112,512]{1,0:T(8,128)(2,1)S(1)} %copy-done), custom_call_target="tpu_custom_call" | custom-call | flops 1233125376 | bytes 2097152 | tf_op jit(solution)/shard_map/pallas_call | solution.py:324
  97.4 0.0 copy-done.1
  97.4 0.8 multiply_subtract_fusion
Async XLA Ops:
  0.6 0.9 copy-start
  1.5 95.8 %copy-start.1 = (f32[112,512]{1,0:T(8,128)S(1)}, f32[112,512]{1,0:T(8,128)}, u32[]{:S(2)}) copy-start(f32[112,512]{1,0:T(8,128)} %param.3) | copy-start | bytes 688132

commit v3 on v2

--- a/solution.py
+++ b/solution.py
@@ -24,6 +24,7 @@
 CUT = 64
 REST = ROWS - CUT
 CHUNKS = ((0, CUT), (CUT, REST))
+NH = len(CHUNKS)
 MESH = pl.DeviceIdType.MESH
 F32 = jnp.float32
 BF16 = jnp.bfloat16
@@ -112,7 +113,7 @@
 
     def partial(dx, same_zh):
         other = slot(dx, same_zh, False)
-        for h in range(2):
+        for h in range(NH):
             arrived(other, h)
         p = other // 2
         rhs = xp[pl.ds(2 * p, 2)].reshape(2 * WIDE, COLS)
@@ -132,7 +133,7 @@
 
     def both(d, same_zh, on_ahead, on_behind):
         lo, hi = slot(-d, same_zh), slot(d, same_zh)
-        for h in range(2):
+        for h in range(NH):
             arrived(lo, h)
             forward(lo, h, on_ahead, False)
             arrived(hi, h)
@@ -140,7 +141,7 @@
 
     def one(dx, same_zh, on_ahead, on_behind):
         s = slot(dx, same_zh)
-        for h in range(2):
+        for h in range(NH):
             arrived(s, h)
             forward(s, h, on_ahead, on_behind)
 
@@ -170,10 +171,10 @@
     both(3, False, False, True)
     partial(-2, False)
     partial(2, False)
-    one(4, False, False, False)
     partial(-4, True)
     partial(-3, False)
     partial(3, False)
+    one(4, False, False, False)
     partial(4, False)
 
 
@@ -215,38 +216,40 @@
     def low(buf, s):
         return buf.at[s, pl.ds(CUT, REST)]
 
-    def spread(buf, n):
-        def to_z(s):
-            for j in range(1, NZ):
-                remote(top(buf, s), top(buf, s), saz.at[n], raz.at[n, zl], (r, y * NZ + z_peer(j))).start()
-
-        def to_y(s):
-            for i in AROUND[1:]:
-                remote(low(buf, s), low(buf, s), sby.at[n], rby.at[n, y], (r, y_peer(i) * NZ + zl)).start()
-
+    def to_z(buf, n, s, oy):
+        for j in range(1, NZ):
+            remote(top(buf, s), top(buf, s), saz.at[n], raz.at[n, zl, oy], (r, y * NZ + z_peer(j))).start()
+
+    def to_y(buf, n, s):
+        for i in AROUND[1:]:
+            remote(low(buf, s), low(buf, s), sby.at[n], rby.at[n, y], (r, y_peer(i) * NZ + zl)).start()
+
+    def spread_own(buf, n):
         for i in AROUND[1:]:
             remote(top(buf, mine), top(buf, mine), say.at[n], ray.at[n, y], (r, y_peer(i) * NZ + zl)).start()
         for j in range(1, NZ):
             remote(low(buf, mine), low(buf, mine), sbz.at[n], rbz.at[n, zl], (r, y * NZ + z_peer(j))).start()
-        to_z(mine)
-        to_y(mine)
-        yield
+        to_z(buf, n, mine, y)
+        to_y(buf, n, mine)
+
+    def spread_low(buf, n):
         for j in range(1, NZ):
             s = slot_of(y, z_peer(j))
             settle(low(buf, s), rbz.at[n, z_peer(j)])
-            to_y(s)
+            to_y(buf, n, s)
+
+    def spread_top(buf, n):
         for i in AROUND[1:]:
             s = slot_of(y_peer(i), zl)
             settle(top(buf, s), ray.at[n, y_peer(i)])
-            to_z(s)
+            to_z(buf, n, s, y_peer(i))
 
     def gathered(buf, n):
         for i in AROUND:
             oy = y_peer(i)
-            if i == 0:
-                for j in range(1, NZ):
-                    settle(buf.at[pl.ds(0, NY), pl.ds(0, CUT)], raz.at[n, z_peer(j)])
-            else:
+            for j in range(1, NZ):
+                settle(top(buf, slot_of(oy, z_peer(j))), raz.at[n, z_peer(j), oy])
+            if i:
                 settle(buf.at[pl.ds(0, NZ), pl.ds(CUT, REST)], rby.at[n, oy])
             yield [slot_of(oy, z) for z in range(NZ)]
 
@@ -259,9 +262,6 @@
     def joined(buf, slots, axis):
         return jnp.concatenate([buf[s] for s in slots], axis=axis)
 
-    steps = spread(gram, 0)
-    next(steps)
-
 
     own = gram.at[mine]
 
@@ -277,37 +277,42 @@
     tile(own, r, ot.at[0], across)
     for i in AROUND[1:]:
         tile(own, r, st.at[0, i], (slot(i, True), c))
+    spread_own(gram, 0)
     tile(own, r, ot.at[1], twin)
-    for _ in steps:
-        pass
+    spread_low(gram, 0)
     s = slot(0, False)
     tile_arrived(s)
     there = bt.at[s, pl.ds(0, ROWS)]
     for i in AROUND[1:]:
         tile(there, s, st.at[1, i], (slot(i, True), c))
     tile(there, s, ct.at[s], twin)
-    for same in (True, False):
+    spread_top(gram, 0)
+    square = jnp.zeros((ROWS, WIDE), F32)
+    for same, half in ((True, zh), (False, 1 - zh)):
         for i in AROUND[1:]:
             s = slot(i, same)
             tile_arrived(s)
             tile(bt.at[s, pl.ds(0, ROWS)], s, ct.at[s], twin)
-    for same in (True, False):
         for i in AROUND:
             tile_arrived(slot(i, same, False))
-
-    square = jnp.zeros((ROWS, WIDE), F32)
-    for slots in gathered(gram, 0):
-        square += jnp.dot(joined(gram, slots, 1), joined(bt, slots, 0), preferred_element_type=F32)
+        for i in range(NY // 2):
+            oy = half * (NY // 2) + i
+            for j in range(1, NZ):
+                settle(top(gram, slot_of(oy, z_peer(j))), raz.at[0, z_peer(j), oy])
+
+            @pl.when(oy != y)
+            def _():
+                settle(gram.at[pl.ds(0, NZ), pl.ds(CUT, REST)], rby.at[0, oy])
+
+            slots = [slot_of(oy, z) for z in range(NZ)]
+            square += jnp.dot(joined(gram, slots, 1), joined(bt, slots, 0), preferred_element_type=F32)
     pol[mine] = (poly_three * gram[mine].astype(F32) + poly_five * square).astype(BF16)
 
 
-    for _ in spread(pol, 1):
-        pass
+    spread_own(pol, 1)
+    spread_low(pol, 1)
+    spread_top(pol, 1)
     yacc[...] = poly_one * xv[...].astype(F32)
-    for slots in gathered(pol, 1):
-        yacc[...] += jnp.dot(joined(pol, slots, 1), joined(xp, slots, 0), preferred_element_type=F32)
-    out_ref[...] = yacc[...]
-
     for cp in started:
         cp.wait_send()
     settle(part.at[pl.ds(0, NY * (NZ - 1)), pl.ds(0, CUT)], spa)
@@ -315,6 +320,10 @@
     settle(sa.at[pl.ds(0, NY - 1)], sqa)
     settle(sb.at[pl.ds(0, NZ - 1)], sqb)
     spread_done(gram, 0)
+    for slots in gathered(pol, 1):
+        yacc[...] += jnp.dot(joined(pol, slots, 1), joined(xp, slots, 0), preferred_element_type=F32)
+    out_ref[...] = yacc[...]
+
     spread_done(pol, 1)
 
 
@@ -339,9 +348,9 @@
             pltpu.VMEM((NR, ROWS, WIDE), BF16),
             pltpu.VMEM((NR, WIDE, WIDE), BF16),
             pltpu.VMEM((ROWS, COLS), F32),
-            dma((NR, 2)), dma((NR, 2)), dma((NR, 2)), dma((NR, 2)), dma((4, 2)),
+            dma((NR, NH)), dma((NR, NH)), dma((NR, NH)), dma((NR, NH)), dma((4, NH)),
             one, one, one, one, one, one, one, one,
-            dma((2, NY)), dma((2, NZ)), dma((2,)), dma((2,)), dma((2, NY)), dma((2, NZ)), dma((2,)), dma((2,)),
+            dma((2, NY)), dma((2, NZ, NY)), dma((2,)), dma((2,)), dma((2, NY)), dma((2, NZ)), dma((2,)), dma((2,)),
             dma((NR,)), dma((2, NX)), dma((NR,)), dma((2,)),
         ],
         compiler_params=pltpu.CompilerParams(

time: 98.3 us -> 96.7 us (0.984)
  Pallas kernels: 95.8 us -> 94.2 us
    pallas_call x1, Pallas kernels: 95.8 us -> 94.2 us  [shards(): pl.pallas_call(kernel, out_shape=jax.ShapeDtypeStruct((ROWS, COLS), F32),...]
where the time goes in v3:
time: 96.7 us; the launch traced here: 96.6 us
  Pallas kernels  94.2 us (97%)
    pallas_call x1, Pallas kernels, shards(): pl.pallas_call(kernel, out_shape=jax.ShapeDtypeStruct((ROWS, COLS), F32),...  94.2 us

profile of v3, /device:TPU:1, one launch (start us, length us, event | category | flops | bytes accessed | tf_op | source)
XLA Modules:
  0.0 96.6 jit_solution(1675349505785504476)
XLA Ops:
  0.6 0.0 copy-start
  0.6 0.9 copy-done
  1.5 0.0 copy-start.1
  1.5 94.2 %shard_map.41 = f32[112,512]{1,0:T(8,128)S(1)} custom-call(bf16[112,512]{1,0:T(8,128)(2,1)S(1)} %copy-done), custom_call_target="tpu_custom_call" | custom-call | flops 1233125376 | bytes 2097152 | tf_op jit(solution)/shard_map/pallas_call | solution.py:333
  95.7 0.0 copy-done.1
  95.7 0.8 multiply_subtract_fusion
Async XLA Ops:
  0.6 0.9 copy-start
  1.5 94.2 %copy-start.1 = (f32[112,512]{1,0:T(8,128)S(1)}, f32[112,512]{1,0:T(8,128)}, u32[]{:S(2)}) copy-start(f32[112,512]{1,0:T(8,128)} %param.3) | copy-start | bytes 688132

commit v4 on v3

--- a/solution.py
+++ b/solution.py
@@ -293,6 +293,7 @@
             s = slot(i, same)
             tile_arrived(s)
             tile(bt.at[s, pl.ds(0, ROWS)], s, ct.at[s], twin)
+    for same, half in ((True, zh), (False, 1 - zh)):
         for i in AROUND:
             tile_arrived(slot(i, same, False))
         for i in range(NY // 2):

time: 96.7 us -> 95.5 us (0.988)
  Pallas kernels: 94.2 us -> 92.9 us
    pallas_call x1, Pallas kernels: 94.2 us -> 92.9 us  [shards(): pl.pallas_call(kernel, out_shape=jax.ShapeDtypeStruct((ROWS, COLS), F32),...]
where the time goes in v4:
time: 95.5 us; the launch traced here: 95.3 us
  Pallas kernels  92.9 us (97%)
    pallas_call x1, Pallas kernels, shards(): pl.pallas_call(kernel, out_shape=jax.ShapeDtypeStruct((ROWS, COLS), F32),...  92.9 us

profile of v4, /device:TPU:1, one launch (start us, length us, event | category | flops | bytes accessed | tf_op | source)
XLA Modules:
  0.0 95.3 jit_solution(8146798725295315805)
XLA Ops:
  0.6 0.0 copy-start
  0.6 0.9 copy-done
  1.5 0.0 copy-start.1
  1.5 92.9 %shard_map.41 = f32[112,512]{1,0:T(8,128)S(1)} custom-call(bf16[112,512]{1,0:T(8,128)(2,1)S(1)} %copy-done), custom_call_target="tpu_custom_call" | custom-call | flops 1233125376 | bytes 2097152 | tf_op jit(solution)/shard_map/pallas_call | solution.py:334
  94.5 0.0 copy-done.1
  94.5 0.8 multiply_subtract_fusion
Async XLA Ops:
  0.6 0.9 copy-start
  1.5 93.0 %copy-start.1 = (f32[112,512]{1,0:T(8,128)S(1)}, f32[112,512]{1,0:T(8,128)}, u32[]{:S(2)}) copy-start(f32[112,512]{1,0:T(8,128)} %param.3) | copy-start | bytes 688132

commit v5 on v4

--- a/solution.py
+++ b/solution.py
@@ -29,6 +29,7 @@
 F32 = jnp.float32
 BF16 = jnp.bfloat16
 AROUND = (0, 1, 7, 2, 6, 3, 5, 4)
+FAR_FIRST = AROUND[:0:-1]
 
 
 def owner_of(slot):
@@ -179,7 +180,7 @@
 
 
     settle(pa.at[pl.ds(0, NZ - 1)], rpa)
-    for i in AROUND:
+    for i in (*FAR_FIRST, 0):
         oy = y_peer(i)
         s = slot_of(oy, zl)
         total = part[s, :CUT].astype(F32)
@@ -221,11 +222,11 @@
             remote(top(buf, s), top(buf, s), saz.at[n], raz.at[n, zl, oy], (r, y * NZ + z_peer(j))).start()
 
     def to_y(buf, n, s):
-        for i in AROUND[1:]:
+        for i in FAR_FIRST:
             remote(low(buf, s), low(buf, s), sby.at[n], rby.at[n, y], (r, y_peer(i) * NZ + zl)).start()
 
     def spread_own(buf, n):
-        for i in AROUND[1:]:
+        for i in FAR_FIRST:
             remote(top(buf, mine), top(buf, mine), say.at[n], ray.at[n, y], (r, y_peer(i) * NZ + zl)).start()
         for j in range(1, NZ):
             remote(low(buf, mine), low(buf, mine), sbz.at[n], rbz.at[n, zl], (r, y * NZ + z_peer(j))).start()
@@ -275,7 +276,7 @@
 
     bt[r, :ROWS] = gram[mine]
     tile(own, r, ot.at[0], across)
-    for i in AROUND[1:]:
+    for i in FAR_FIRST:
         tile(own, r, st.at[0, i], (slot(i, True), c))
     spread_own(gram, 0)
     tile(own, r, ot.at[1], twin)
@@ -283,7 +284,7 @@
     s = slot(0, False)
     tile_arrived(s)
     there = bt.at[s, pl.ds(0, ROWS)]
-    for i in AROUND[1:]:
+    for i in FAR_FIRST:
         tile(there, s, st.at[1, i], (slot(i, True), c))
     tile(there, s, ct.at[s], twin)
     spread_top(gram, 0)

time: 95.5 us -> 96.4 us (level)
  the two profiles are of different devices: /device:TPU:1 before, /device:TPU:14 now
where the time goes in v5:
time: 96.4 us; the launch traced here: 96.3 us
  Pallas kernels  93.9 us (97%)
    pallas_call x1, Pallas kernels, shards(): pl.pallas_call(kernel, out_shape=jax.ShapeDtypeStruct((ROWS, COLS), F32),...  93.9 us

profile of v5, /device:TPU:14, one launch (start us, length us, event | category | flops | bytes accessed | tf_op | source)
XLA Modules:
  0.0 96.3 jit_solution(5941684629128857233)
XLA Ops:
  0.6 0.0 copy-start
  0.6 0.9 copy-done
  1.5 0.0 copy-start.1
  1.5 93.9 %shard_map.41 = f32[112,512]{1,0:T(8,128)S(1)} custom-call(bf16[112,512]{1,0:T(8,128)(2,1)S(1)} %copy-done), custom_call_target="tpu_custom_call" | custom-call | flops 1233125376 | bytes 2097152 | tf_op jit(solution)/shard_map/pallas_call | solution.py:335
  95.5 0.0 copy-done.1
  95.5 0.8 multiply_subtract_fusion
Async XLA Ops:
  0.6 0.9 copy-start
  1.5 93.9 %copy-start.1 = (f32[112,512]{1,0:T(8,128)S(1)}, f32[112,512]{1,0:T(8,128)}, u32[]{:S(2)}) copy-start(f32[112,512]{1,0:T(8,128)} %param.3) | copy-start | bytes 688132
